TPU v7x, 32 devices: a whole 2x2x4 slice. The times are simulated.
32 devices in a mesh: dp: 8 (over z, core), tensor: 4 (over y, x).
Axes of the slice: x: 2, y: 2, z: 4, core: 2. Of those that a mesh axis runs over, the one named last changes fastest.
Arguments:
- patches: bfloat16 [8192, 3200], P('dp', 'tensor'), may hold values from -40 to 40
- encoder_row: int32 [8192], P('dp'), may hold values from 0 to 8191, as said below
- norm_gain: bfloat16 [3200], P('tensor'), may hold values from 0.5 to 1.5
- joint_weight: bfloat16 [3200, 6144], P(None, 'tensor'), may hold values from -8 to 8
- out_weight: bfloat16 [2048, 3200], P(None, 'tensor'), may hold values from -0.1875 to 0.1875
- layer_scale: bfloat16 [3200], P('tensor'), may hold values from 1 to 8
- pos_embed: bfloat16 [1024, 3200], P(None, 'tensor'), may hold values from -3 to 3
Outputs:
- encoded: bfloat16 [8192, 3200], P('dp', 'tensor')
Inputs may be any that keep to these rules, and one draw needn't show every extreme that they name: `encoder_row`: A bijection from the rows of patches onto the encoder rows; device d's encoder batch is rows d * 1024 to (d + 1) * 1024 - 1. The rows of each aligned block of 1024 rows of the packed stream (one tile) map onto one aligned block of 1024 encoder rows, and a row's encoder row is congruent to its shard's index modulo 8.
All inputs are finite; a program needn't handle non-finite values.
Results may differ from a plain program's by a relative error of at most 0.0058.
Values may be sent and summed in bfloat16 or wider, within the bound.
A program may use at most 128 MiB of HBM per device.

v0:
```python
import jax
import jax.numpy as jnp
from jax import lax
from jax.sharding import PartitionSpec as P

HD = 128
UNIT = 1024


epsilon = 1e-06


def local(patches, encoder_row, norm_gain, joint_weight, out_weight, layer_scale, pos_embed):
    peer_count = lax.axis_size("dp")
    row_count, col_count = patches.shape
    per_peer = row_count // peer_count
    target_dev = encoder_row // row_count
    target_row = encoder_row % row_count
    send_slot = target_dev * per_peer + target_row // peer_count
    send_order = (
        jnp.zeros((row_count,), jnp.int32).at[send_slot].set(jnp.arange(row_count, dtype=jnp.int32))
    )
    outgoing = patches[send_order].reshape(peer_count, per_peer, col_count)
    arrived = lax.all_to_all(outgoing, "dp", split_axis=0, concat_axis=0, tiled=True)
    block_len = UNIT
    block_count = row_count // block_len
    routed = (
        jnp.transpose(arrived, (1, 0, 2))
        .reshape(block_count, block_len, col_count)
        .astype(jnp.float32)
    )
    mine = (
        (routed + pos_embed.astype(jnp.float32)[None])
        .astype(jnp.bfloat16)
        .reshape(row_count, col_count)
    )
    own_feats = mine.astype(jnp.float32)
    local_heads = joint_weight.shape[1] // (3 * HD)
    full_rows, full_gain = (
        lax.all_gather(mine, "tensor", axis=1, tiled=True),
        lax.all_gather(norm_gain, "tensor", axis=0, tiled=True),
    )
    full_feats = full_rows.astype(jnp.float32)
    square_mean = jnp.mean(full_feats * full_feats, axis=-1, keepdims=True)
    scaled = (full_feats * full_gain.astype(jnp.float32)).astype(jnp.bfloat16)
    joint_proj = jnp.dot(scaled, joint_weight, preferred_element_type=jnp.float32)
    joint_proj = (joint_proj * lax.rsqrt(square_mean + epsilon)).astype(jnp.bfloat16)
    joint_proj = joint_proj.reshape(block_count, block_len, local_heads, 3, HD)
    queries = joint_proj[:, :, :, 0]
    key_vecs = joint_proj[:, :, :, 1]
    values = joint_proj[:, :, :, 2]
    scores = jnp.einsum(
        "bqhd,bkhd->bhqk", queries, key_vecs, preferred_element_type=jnp.float32
    ) * HD ** (-0.5)
    row_peak = jnp.max(scores, axis=-1, keepdims=True)
    exponent = jnp.exp(scores - row_peak)
    weights = (exponent / jnp.sum(exponent, axis=-1, keepdims=True)).astype(jnp.bfloat16)
    attended = jnp.einsum("bhqk,bkhd->bqhd", weights, values, preferred_element_type=jnp.float32)
    attended = attended.astype(jnp.bfloat16).reshape(row_count, local_heads * HD)
    merged = jnp.dot(
        lax.all_gather(attended, "tensor", axis=1, tiled=True),
        out_weight,
        preferred_element_type=jnp.float32,
    )
    result = (own_feats + layer_scale.astype(jnp.float32) * merged).astype(jnp.bfloat16)
    leaving = jnp.transpose(result.reshape(per_peer, peer_count, col_count), (1, 0, 2))
    returned = lax.all_to_all(leaving, "dp", split_axis=0, concat_axis=0, tiled=True)
    return returned.reshape(row_count, col_count)[send_slot]


def solution(mesh):
    placed = (
        P("dp", "tensor"),
        P("dp"),
        P("tensor"),
        P(None, "tensor"),
        P(None, "tensor"),
        P("tensor"),
        P(None, "tensor"),
    )
    return jax.shard_map(
        local, mesh=mesh, in_specs=placed, out_specs=P("dp", "tensor"), check_vma=False
    )
```

profile of v0, /device:TPU:0, one launch (start us, length us, event | category | flops | bytes accessed | tf_op | source)
XLA Modules:
  0.0 353.4 jit_solution(9436105055787258519)
XLA Ops:
  7.4 4.3 %scatter_custom_fusion = s32[1024]{0:T(1024)S(1)} fusion(s32[1024]{0:T(1024)S(1)} %get-tuple-element.6, s32[1024]{0:T(1024)S(1)} %iota.3, s32[]{:T(128)} %constant.40.clone.1), kind=kCustom, calls=%fused_computation.47 | custom fusion | bytes 4100 | tf_op jit(solution)/shard_map/scatter | solution.py:21
  11.7 3.8 %copy.27 = bf16[1024,800]{1,0:T(8,128)(2,1)} copy(bf16[1024,800]{0,1:T(8,128)(2,1)} %param.7) | data formatting | bytes 3276800 | tf_op args[0]
  15.5 7.5 %gather_fusion = bf16[1024,800]{1,0:T(8,128)(2,1)} fusion(bf16[1024,800]{1,0:T(8,128)(2,1)} %copy.27, s32[1024]{0:T(1024)S(1)} %fusion.22), kind=kCustom, calls=%fused_computation | custom fusion | bytes 3280896 | tf_op jit(solution)/shard_map/gather | solution.py:23
  23.0 3.7 %copy.28 = bf16[8,128,800]{1,2,0:T(8,128)(2,1)} copy(bf16[8,128,800]{2,1,0:T(8,128)(2,1)} %bitcast.35) | data formatting | bytes 3276800 | tf_op jit(solution)/shard_map/reshape | solution.py:23
  26.7 45.6 %all_to_all.10 = bf16[8,128,800]{1,2,0:T(8,128)(2,1)S(1)} all-to-all(bf16[8,128,800]{1,2,0:T(8,128)(2,1)} %copy.28), channel_id=1, replica_groups=mesh['dp'=8,'tensor'=4] {'dp'}, dimensions={0} | all-to-all | bytes 3276800 | tf_op jit(solution)/shard_map/all_to_all | solution.py:24
  74.2 4.5 %copy.29 = f32[128,8,800]{2,1,0:T(8,128)} copy(f32[128,8,800]{0,2,1:T(8,128)} %convert_bitcast_fusion) | data formatting | bytes 6553600 | tf_op jit(solution)/shard_map/convert_element_type | solution.py:30
  78.7 4.9 %copy.30 = f32[1024,800]{0,1:T(8,128)} copy(f32[1024,800]{1,0:T(8,128)} %bitcast.32) | data formatting | bytes 6553600 | tf_op jit(solution)/shard_map/convert_element_type | solution.py:30
  83.6 4.2 %add_convert_fusion.1 = bf16[1024,800]{0,1:T(8,128)(2,1)} fusion(f32[1024,800]{0,1:T(8,128)} %copy.30, bf16[1024,800]{0,1:T(8,128)(2,1)} %param.13), kind=kLoop, calls=%fused_computation.19 | loop fusion | flops 2457600 | bytes 6553600 | tf_op jit(solution)/shard_map/convert_element_type | solution.py:34
  89.4 10.2 %all-reduce = bf16[3200]{0:T(1024)(128)(2,1)S(1)} all-reduce(bf16[3200]{0:T(1024)(128)(2,1)S(1)} %dynamic-update-slice), channel_id=1, replica_groups=mesh['dp'=8,'tensor'=4] {'tensor'}, use_global_device_ids=true, to_apply=%add | all-reduce | flops 3200 | bytes 12800
  99.6 59.7 %all-gather.3.cloned.1.call-done = bf16[1024,3200]{0,1:T(8,128)(2,1)} async-done(((bf16[1024,800]{0,1:T(8,128)(2,1)}), bf16[1024,3200]{0,1:T(8,128)(2,1)}) %all-gather.3.cloned.1.call-update) | async-done | bytes 6553616 | tf_op jit(solution)/shard_map/all_gather | solution.py:40
  159.3 4.4 %fusion.5 = f32[1024]{0:T(1024)S(1)} fusion(bf16[1024,3200]{0,1:T(8,128)(2,1)} %all-gather.3.cloned.1.call-done), kind=kLoop, calls=%fused_computation.11 | loop fusion | flops 9829376 | bytes 6557696 | tf_op jit(solution)/shard_map/reduce_sum | solution.py:44
  164.0 14.8 %multiply_convert_fusion = bf16[1024,1536]{1,0:T(8,128)(2,1)} fusion(bf16[3200,1536]{1,0:T(8,128)(2,1)} %param.10, bf16[1024,3200]{0,1:T(8,128)(2,1)S(1)} %copy-done.1, f32[3200]{0:T(1024)S(1)} %convert_element_type.59, f32[1024]{0:T(1024)S(1)} %add_rsqrt_fusion), kind=kOutput, calls=%fused_computation.16 | convolution fusion | flops 10079305728 | bytes 19546624 | tf_op jit(solution)/shard_map/dot_general | solution.py:46
  178.8 4.6 %copy.31 = bf16[1024,1536]{0,1:T(8,128)(2,1)} copy(bf16[1024,1536]{1,0:T(8,128)(2,1)} %multiply_convert_fusion) | data formatting | bytes 6291456 | tf_op jit(solution)/shard_map/convert_element_type | solution.py:47
  183.5 9.6 %fusion.14 = f32[4,1024,1024]{1,2,0:T(8,128)} fusion(bf16[1,1024,4,3,128]{1,4,3,2,0:T(8,128)(2,1)} %bitcast.33), kind=kOutput, calls=%fused_computation.22 | convolution fusion | flops 1073741824 | bytes 18874368 | tf_op jit(solution)/shard_map/bqhd,bkhd->bhqk/dot_general | solution.py:52
  193.1 12.6 %fusion.32 = f32[4,1024]{1,0:T(4,128)S(1)} fusion(f32[4,1024,1024]{1,2,0:T(8,128)} %fusion.14), kind=kOutput, calls=%fused_computation.52 | output fusion | flops 16778240 | bytes 16793600 | tf_op jit(solution)/shard_map/sub | solution.py:56
  205.7 14.5 %fusion.13 = bf16[4,128,1024]{2,1,0:T(8,128)(2,1)} fusion(f32[4,1024]{1,0:T(4,128)S(1)} %fusion.32, bf16[1,1024,4,3,128]{1,4,3,2,0:T(8,128)(2,1)} %bitcast.34, f32[4,1024,1024]{1,2,0:T(8,128)} %fusion.14), kind=kOutput, calls=%fused_computation.20 | convolution fusion | flops 1095242752 | bytes 35667968 | tf_op jit(solution)/shard_map/bhqk,bkhd->bqhd/dot_general | solution.py:58
  220.3 52.8 %all-gather.5.cloned.1.call-done = bf16[1024,2048]{0,1:T(8,128)(2,1)} async-done(((bf16[1024,512]{0,1:T(8,128)(2,1)}), bf16[1024,2048]{0,1:T(8,128)(2,1)}) %all-gather.5.cloned.1.call-update) | async-done | bytes 4194320 | tf_op jit(solution)/shard_map/all_gather | solution.py:61
  273.1 7.1 %add_convert_fusion = bf16[1024,800]{0,1:T(8,128)(2,1)} fusion(bf16[1024,800]{0,1:T(8,128)(2,1)} %add_convert_fusion.1, bf16[2048,800]{0,1:T(8,128)(2,1)S(1)} %copy-done, bf16[1024,2048]{0,1:T(8,128)(2,1)} %all-gather.5.cloned.1.call-done, f32[800]{0:T(1024)S(1)} %convert_element_type.57), kind=kOutput, calls=%fused_computation.18 | convolution fusion | flops 3358720000 | bytes 10751104 | tf_op jit(solution)/shard_map/dot_general | solution.py:60
  280.2 3.7 %copy.36 = bf16[1024,800]{1,0:T(8,128)(2,1)} copy(bf16[1024,800]{0,1:T(8,128)(2,1)} %add_convert_fusion) | data formatting | bytes 3276800 | tf_op jit(solution)/shard_map/convert_element_type | solution.py:65
  283.9 3.7 %copy.37 = bf16[8,128,800]{1,2,0:T(8,128)(2,1)} copy(bf16[8,128,800]{2,0,1:T(8,128)(2,1)} %bitcast.36) | data formatting | bytes 3276800 | tf_op jit(solution)/shard_map/transpose | solution.py:66
  287.7 43.9 %all_to_all.11 = bf16[8,128,800]{1,2,0:T(8,128)(2,1)} all-to-all(bf16[8,128,800]{1,2,0:T(8,128)(2,1)} %copy.37), channel_id=1, replica_groups=mesh['dp'=8,'tensor'=4] {'dp'}, dimensions={0} | all-to-all | bytes 3276800 | tf_op jit(solution)/shard_map/all_to_all | solution.py:67
  331.6 3.7 %copy.38 = bf16[8,128,800]{2,1,0:T(8,128)(2,1)} copy(bf16[8,128,800]{1,2,0:T(8,128)(2,1)} %all_to_all.11) | data formatting | bytes 3276800 | tf_op jit(solution)/shard_map/all_to_all | solution.py:67
  335.3 7.5 %gather_fusion.1 = bf16[1024,800]{1,0:T(8,128)(2,1)} fusion(bf16[1024,800]{1,0:T(8,128)(2,1)} %bitcast.31, s32[1024]{0:T(1024)S(1)} %get-tuple-element.5), kind=kCustom, calls=%fused_computation.1 | custom fusion | bytes 3280896 | tf_op jit(solution)/shard_map/gather | solution.py:68
  342.8 3.7 %copy.39 = bf16[1024,800]{0,1:T(8,128)(2,1)} copy(bf16[1024,800]{1,0:T(8,128)(2,1)} %gather_fusion.1) | data formatting | bytes 3276800 | tf_op jit(solution)/shard_map/gather | solution.py:68
  (24 shorter events, 4.1 us)
Async XLA Ops:
  6.5 266.6 %copy-start = (bf16[2048,800]{0,1:T(8,128)(2,1)S(1)}, bf16[2048,800]{0,1:T(8,128)(2,1)}, u32[]{:S(2)}) copy-start(bf16[2048,800]{0,1:T(8,128)(2,1)} %param.11) | copy-start | bytes 9830404
  6.5 152.7 %all-gather.3.cloned.1.call-start = ((), (), s32[]{:S(2)}) async-start(), calls=%async_computation.2 | async-start | bytes 8192000 | tf_op jit(solution)/shard_map/all_gather | solution.py:40
  83.6 4.3 %copy-start.4 = (u32[32]{0:T(128)S(1)}, u32[32]{0:T(128)}, u32[]{:S(2)}) copy-start(u32[32]{0:T(128)} %constant.56) | copy-start | bytes 388
  83.6 5.6 %copy-start.3 = (bf16[800]{0:T(1024)(128)(2,1)S(1)}, bf16[800]{0:T(1024)(128)(2,1)}, u32[]{:S(2)}) copy-start(bf16[800]{0:T(1024)(128)(2,1)} %param.9) | copy-start | bytes 4804
  87.8 185.2 %all-gather.5.cloned.1.call-start = ((), (), s32[]{:S(2)}) async-start(), calls=%async_computation.3 | async-start | bytes 5242880 | tf_op jit(solution)/shard_map/all_gather | solution.py:61
  159.3 4.7 %copy-start.1 = (bf16[1024,3200]{0,1:T(8,128)(2,1)S(1)}, bf16[1024,3200]{0,1:T(8,128)(2,1)}, u32[]{:S(2)}) copy-start(bf16[1024,3200]{0,1:T(8,128)(2,1)} %all-gather.3.cloned.1.call-done) | copy-start | bytes 19660804
  205.7 14.6 %copy-start.2 = (bf16[800]{0:T(1024)(128)(2,1)S(1)}, bf16[800]{0:T(1024)(128)(2,1)}, u32[]{:S(2)}) copy-start(bf16[800]{0:T(1024)(128)(2,1)} %param.12) | copy-start | bytes 4804
Sparse Core Ops, SparseCore 0:
  88.0 71.2 all-gather.2
  220.4 52.6 all-gather.4
where the time goes:
time: 354 us; the launch traced here: 353 us
  waiting for transfers between devices  113 us (32%)
  blocking collectives  99.6 us (28%)
  local copies, waits for them, and re-layouts  57 us (16%)
  matrix products  46.1 us (13%)
  other arithmetic  24 us (7%)
  between operations  14.1 us (4%)
    all_gather x1, waiting for transfers between devices, local(): lax.all_gather(mine, 'tensor', axis=1, tiled=True)  59.7 us
    all_gather x1, waiting for transfers between devices, local(): lax.all_gather(attended, 'tensor', axis=1, tiled=True)  52.8 us
    all_to_all x1, blocking collectives, local(): lax.all_to_all(outgoing, 'dp', split_axis=0, concat_axis=0, tiled=True)  45.6 us
    all_to_all x1, blocking collectives, local(): lax.all_to_all(leaving, 'dp', split_axis=0, concat_axis=0, tiled=True)  43.9 us
    dot_general x1, matrix products, local(): jnp.dot(scaled, joint_weight, preferred_element_type=jnp.float32)  14.8 us
    dot_general x1, matrix products, local(): jnp.einsum('bhqk,bkhd->bqhd', weights, values, preferred_element_type=jnp...  14.5 us
    sub x1, other arithmetic, local(): exponent = jnp.exp(scores - row_peak)  12.6 us
    gather x2, local copies, waits for them, and re-layouts, local(): return returned.reshape(row_count, col_count)[send_slot]  11.2 us
  transfers between devices with their start and end apart: 2, of which 2 were waited for; matrix products, arithmetic and copies ran while one was open for 0% of the time, Pallas kernels for 0%

commit v1 on v0

v1 whole, which is shorter than its diff:
```python
import functools

import jax
import jax.numpy as jnp
from jax import lax
from jax.sharding import PartitionSpec as P

HD = 128
UNIT = 1024
EPS = 1e-06


def plain(patches, encoder_row, norm_gain, joint_weight, out_weight, layer_scale, pos_embed):
    peers = lax.axis_size("dp")
    rows, cols = patches.shape
    heads = joint_weight.shape[1] // (3 * HD)
    tiles = rows // UNIT
    per = UNIT // peers

    def swap(x):
        wide = x.shape[-1]
        x = x.reshape(peers, tiles * per, wide)
        return lax.all_to_all(x, "dp", split_axis=0, concat_axis=0, tiled=True)

    pos = pos_embed[encoder_row % UNIT].astype(jnp.float32)
    mine = (patches.astype(jnp.float32) + pos).astype(jnp.bfloat16)
    tile_rows = swap(mine).reshape(peers, tiles, per, cols)
    tile_rows = jnp.swapaxes(tile_rows, 0, 1).reshape(rows, cols)
    full = lax.all_gather(tile_rows, "tensor", axis=1, tiled=True).astype(jnp.float32)
    gain = lax.all_gather(norm_gain, "tensor", axis=0, tiled=True).astype(jnp.float32)
    square_mean = jnp.mean(full * full, axis=-1, keepdims=True)
    scaled = (full * gain).astype(jnp.bfloat16)
    proj = jnp.dot(scaled, joint_weight, preferred_element_type=jnp.float32)
    proj = (proj * lax.rsqrt(square_mean + EPS)).astype(jnp.bfloat16)
    proj = proj.reshape(tiles, UNIT, heads, 3, HD)
    q, k, v = proj[:, :, :, 0], proj[:, :, :, 1], proj[:, :, :, 2]
    scores = jnp.einsum("bqhd,bkhd->bhqk", q, k, preferred_element_type=jnp.float32) * HD ** (-0.5)
    e = jnp.exp(scores - jnp.max(scores, axis=-1, keepdims=True))
    weights = (e / jnp.sum(e, axis=-1, keepdims=True)).astype(jnp.bfloat16)
    att = jnp.einsum("bhqk,bkhd->bqhd", weights, v, preferred_element_type=jnp.float32)
    att = att.astype(jnp.bfloat16).reshape(tiles, peers, per, heads * HD)
    back = swap(jnp.swapaxes(att, 0, 1).reshape(rows, heads * HD)).reshape(rows, heads * HD)
    back = lax.all_gather(back, "tensor", axis=1, tiled=True)
    merged = jnp.dot(back, out_weight, preferred_element_type=jnp.float32)
    return (mine.astype(jnp.float32) + layer_scale.astype(jnp.float32) * merged).astype(jnp.bfloat16)


def solution(mesh):
    body = plain
    placed = (
        P("dp", "tensor"),
        P("dp"),
        P("tensor"),
        P(None, "tensor"),
        P(None, "tensor"),
        P("tensor"),
        P(None, "tensor"),
    )
    return jax.shard_map(
        body, mesh=mesh, in_specs=placed, out_specs=P("dp", "tensor"), check_vma=False
    )
```

time: 354 us -> 304 us (0.86)
  local copies, waits for them, and re-layouts: 57 us -> 26.3 us
  blocking collectives: 99.6 us -> 86.6 us
  other arithmetic: 24 us -> 19.3 us
    convert_element_type x4 -> x1, local copies, waits for them, and re-layouts: 17.8 us -> 4.65 us  [plain(): proj = (proj * lax.rsqrt(square_mean + EPS)).astype(jnp.bfloat16)]
    all_to_all x2, blocking collectives: 89.5 us -> 76.5 us  [swap(): return lax.all_to_all(x, 'dp', split_axis=0, concat_axis=0, tiled=True)]
    gather x3 -> x2, local copies, waits for them, and re-layouts: 18.7 us -> 11.2 us  [plain(): pos = pos_embed[encoder_row % UNIT].astype(jnp.float32)]
    convert_element_type x4 -> x2, other arithmetic: 6.17 us -> 0.01 us  [the longest x1 0.01 us: plain(): lax.all_gather(norm_gain, 'tensor', axis=0, tiled=True).astype(jnp.float32)]
    scatter x1 -> x0, local copies, waits for them, and re-layouts: 4.31 us -> none  [local(): jnp.zeros((row_count,), jnp.int32).at[send_slot]]
    transpose x1 -> x0, local copies, waits for them, and re-layouts: 3.74 us -> none  [local(): jnp.transpose(result.reshape(per_peer, peer_count, col_count), (1, 0, 2))]
    reshape x1 -> x0, local copies, waits for them, and re-layouts: 3.7 us -> none  [local(): outgoing = patches[send_order].reshape(peer_count, per_peer, col_count)]
where the time goes in v1:
time: 304 us; the launch traced here: 303 us
  waiting for transfers between devices  110 us (36%)
  blocking collectives  86.6 us (28%)
  matrix products  46.4 us (15%)
  local copies, waits for them, and re-layouts  26.3 us (9%)
  other arithmetic  19.3 us (6%)
  between operations  14.1 us (5%)
    all_to_all x2, blocking collectives, swap(): return lax.all_to_all(x, 'dp', split_axis=0, concat_axis=0, tiled=True)  76.5 us
    all_gather x1, waiting for transfers between devices, plain(): lax.all_gather(tile_rows, 'tensor', axis=1, tiled=True).astype(jnp.float32)  59.7 us
    all_gather x1, waiting for transfers between devices, plain(): back = lax.all_gather(back, 'tensor', axis=1, tiled=True)  50.6 us
    dot_general x1, matrix products, plain(): proj = jnp.dot(scaled, joint_weight, preferred_element_type=jnp.float32)  14.8 us
    dot_general x1, matrix products, plain(): jnp.einsum('bhqk,bkhd->bqhd', weights, v, preferred_element_type=jnp.floa...  14.5 us
    sub x1, other arithmetic, plain(): e = jnp.exp(scores - jnp.max(scores, axis=-1, keepdims=True))  12.6 us
    gather x2, local copies, waits for them, and re-layouts, plain(): pos = pos_embed[encoder_row % UNIT].astype(jnp.float32)  11.2 us
    unnamed x1, blocking collectives  10.2 us
  transfers between devices with their start and end apart: 2, of which 2 were waited for; matrix products, arithmetic and copies ran while one was open for 0% of the time, Pallas kernels for 0%

profile of v1, /device:TPU:0, one launch (start us, length us, event | category | flops | bytes accessed | tf_op | source)
XLA Modules:
  0.0 303.2 jit_solution(14297218232632308507)
XLA Ops:
  6.5 3.9 %copy.30 = bf16[1024,800]{1,0:T(8,128)(2,1)} copy(bf16[1024,800]{0,1:T(8,128)(2,1)} %param.13) | data formatting | bytes 3276800 | tf_op args[6]
  10.5 7.5 %gather_fusion = bf16[1024,800]{1,0:T(8,128)(2,1)} fusion(bf16[1024,800]{1,0:T(8,128)(2,1)} %copy.30, s32[1024]{0:T(1024)S(1)} %fusion.21), kind=kCustom, calls=%fused_computation | custom fusion | bytes 3280896 | tf_op jit(solution)/shard_map/gather | solution.py:25
  18.0 3.7 %copy.31 = bf16[1024,800]{0,1:T(8,128)(2,1)} copy(bf16[1024,800]{1,0:T(8,128)(2,1)} %gather_fusion) | data formatting | bytes 3276800 | tf_op jit(solution)/shard_map/gather | solution.py:25
  21.7 2.3 copy_bitcast_fusion.1
  24.0 45.4 %all_to_all.10 = bf16[8,128,800]{1,2,0:T(8,128)(2,1)S(1)} all-to-all(bf16[8,128,800]{1,2,0:T(8,128)(2,1)S(1)} %copy_bitcast_fusion.1), channel_id=1, replica_groups=mesh['dp'=8,'tensor'=4] {'dp'}, dimensions={0} | all-to-all | bytes 3276800 | tf_op jit(solution)/shard_map/all_to_all | solution.py:23
  69.4 1.4 copy_bitcast_fusion
  70.8 0.0 all-gather.5.cloned.1.call-start
  70.9 0.6 dynamic-slice
  72.1 0.2 dynamic-update-slice
  72.4 10.2 %all-reduce = bf16[3200]{0:T(1024)(128)(2,1)S(1)} all-reduce(bf16[3200]{0:T(1024)(128)(2,1)S(1)} %dynamic-update-slice), channel_id=1, replica_groups=mesh['dp'=8,'tensor'=4] {'tensor'}, use_global_device_ids=true, to_apply=%add | all-reduce | flops 3200 | bytes 12800
  82.5 59.7 %all-gather.3.cloned.1.call-done = bf16[1024,3200]{0,1:T(8,128)(2,1)} async-done(((bf16[1024,800]{0,1:T(8,128)(2,1)}), bf16[1024,3200]{0,1:T(8,128)(2,1)}) %all-gather.3.cloned.1.call-update) | async-done | bytes 6553616 | tf_op jit(solution)/shard_map/all_gather | solution.py:29
  142.3 4.4 %fusion.5 = f32[1024]{0:T(1024)S(1)} fusion(bf16[1024,3200]{0,1:T(8,128)(2,1)} %all-gather.3.cloned.1.call-done), kind=kLoop, calls=%fused_computation.9 | loop fusion | flops 9829376 | bytes 6557696 | tf_op jit(solution)/shard_map/reduce_sum | solution.py:31
  146.7 0.4 copy-done.1
  147.0 14.8 %multiply_convert_fusion = bf16[1024,1536]{1,0:T(8,128)(2,1)} fusion(bf16[3200,1536]{1,0:T(8,128)(2,1)} %param.10, bf16[1024,3200]{0,1:T(8,128)(2,1)S(1)} %copy-done.1, f32[3200]{0:T(1024)S(1)} %convert_element_type.49, f32[1024]{0:T(1024)S(1)} %add_rsqrt_fusion), kind=kOutput, calls=%fused_computation.14 | convolution fusion | flops 10079305728 | bytes 19546624 | tf_op jit(solution)/shard_map/dot_general | solution.py:33
  161.8 4.6 %copy.34 = bf16[1024,1536]{0,1:T(8,128)(2,1)} copy(bf16[1024,1536]{1,0:T(8,128)(2,1)} %multiply_convert_fusion) | data formatting | bytes 6291456 | tf_op jit(solution)/shard_map/convert_element_type | solution.py:34
  166.5 9.6 %fusion.14 = f32[4,1024,1024]{1,2,0:T(8,128)} fusion(bf16[1,1024,4,3,128]{1,4,3,2,0:T(8,128)(2,1)} %bitcast.38), kind=kOutput, calls=%fused_computation.21 | convolution fusion | flops 1073741824 | bytes 18874368 | tf_op jit(solution)/shard_map/bqhd,bkhd->bhqk/dot_general | solution.py:37
  176.1 12.6 %fusion.26 = f32[4,1024]{1,0:T(4,128)S(1)} fusion(f32[4,1024,1024]{1,2,0:T(8,128)} %fusion.14), kind=kOutput, calls=%fused_computation.35 | output fusion | flops 16778240 | bytes 16793600 | tf_op jit(solution)/shard_map/sub | solution.py:38
  188.7 14.5 %fusion.13 = bf16[4,128,1024]{2,1,0:T(8,128)(2,1)} fusion(f32[4,1024]{1,0:T(4,128)S(1)} %fusion.26, bf16[1,1024,4,3,128]{1,4,3,2,0:T(8,128)(2,1)} %bitcast.39, f32[4,1024,1024]{1,2,0:T(8,128)} %fusion.14), kind=kOutput, calls=%fused_computation.19 | convolution fusion | flops 1095242752 | bytes 35667968 | tf_op jit(solution)/shard_map/bhqk,bkhd->bqhd/dot_general | solution.py:40
  203.2 1.5 copy.47
  204.7 0.1 copy.39
  204.9 31.1 %all_to_all.11 = bf16[8,128,512]{1,2,0:T(8,128)(2,1)} all-to-all(bf16[8,128,512]{1,2,0:T(8,128)(2,1)S(1)} %copy.39), channel_id=1, replica_groups=mesh['dp'=8,'tensor'=4] {'dp'}, dimensions={0} | all-to-all | bytes 2097152 | tf_op jit(solution)/shard_map/all_to_all | solution.py:23
  236.0 2.3 copy.40
  238.3 50.6 %all-gather.5.cloned.1.call-done = bf16[1024,2048]{1,0:T(8,128)(2,1)} async-done(((bf16[1024,512]{1,0:T(8,128)(2,1)}), bf16[1024,2048]{1,0:T(8,128)(2,1)}) %all-gather.5.cloned.1.call-update) | async-done | bytes 4194320 | tf_op jit(solution)/shard_map/all_gather | solution.py:43
  288.9 7.5 %add_convert_fusion = bf16[1024,800]{0,1:T(8,128)(2,1)} fusion(bf16[1024,2048]{1,0:T(8,128)(2,1)} %all-gather.5.cloned.1.call-done, bf16[2048,800]{0,1:T(8,128)(2,1)S(1)} %copy-done, f32[800]{0:T(1024)S(1)} %convert_element_type.47, bf16[1024,800]{0,1:T(8,128)(2,1)} %copy.31, bf16[1024,800]{0,1:T(8,128)(2,1)} %param.7), kind=kOutput, calls=%fused_computation.15 | convolution fusion | flops 3361996800 | bytes 12389504 | tf_op jit(solution)/shard_map/dot_general | solution.py:44
  (19 shorter events, 0.1 us)
Async XLA Ops:
  6.5 282.4 %copy-start = (bf16[2048,800]{0,1:T(8,128)(2,1)S(1)}, bf16[2048,800]{0,1:T(8,128)(2,1)}, u32[]{:S(2)}) copy-start(bf16[2048,800]{0,1:T(8,128)(2,1)} %param.11) | copy-start | bytes 9830404
  6.5 3.9 %copy-start.2 = (s32[1024]{0:T(1024)S(1)}, s32[1024]{0:T(1024)}, u32[]{:S(2)}) copy-start(s32[1024]{0:T(1024)} %param.8) | copy-start | bytes 12292
  6.5 135.7 %all-gather.3.cloned.1.call-start = ((), (), s32[]{:S(2)}) async-start(), calls=%async_computation.2 | async-start | bytes 8192000 | tf_op jit(solution)/shard_map/all_gather | solution.py:29
  69.4 1.5 copy-start.5
  69.4 2.7 copy-start.4
  70.8 218.1 %all-gather.5.cloned.1.call-start = ((), (), s32[]{:S(2)}) async-start(), calls=%async_computation.3 | async-start | bytes 5242880 | tf_op jit(solution)/shard_map/all_gather | solution.py:43
  142.3 4.7 %copy-start.1 = (bf16[1024,3200]{0,1:T(8,128)(2,1)S(1)}, bf16[1024,3200]{0,1:T(8,128)(2,1)}, u32[]{:S(2)}) copy-start(bf16[1024,3200]{0,1:T(8,128)(2,1)} %all-gather.3.cloned.1.call-done) | copy-start | bytes 19660804
  204.7 33.6 %copy-start.3 = (bf16[800]{0:T(1024)(128)(2,1)S(1)}, bf16[800]{0:T(1024)(128)(2,1)}, u32[]{:S(2)}) copy-start(bf16[800]{0:T(1024)(128)(2,1)} %param.12) | copy-start | bytes 4804
Sparse Core Ops, SparseCore 0:
  70.9 71.2 all-gather.2
  238.4 50.4 all-gather.4

commit v2 on v1

--- a/solution.py
+++ b/solution.py
@@ -1,13 +1,14 @@
-import functools
-
 import jax
 import jax.numpy as jnp
 from jax import lax
+from jax.experimental import pallas as pl
+from jax.experimental.pallas import tpu as pltpu
 from jax.sharding import PartitionSpec as P
 
 HD = 128
 UNIT = 1024
 EPS = 1e-06
+MESH = pl.DeviceIdType.MESH
 
 
 def plain(patches, encoder_row, norm_gain, joint_weight, out_weight, layer_scale, pos_embed):
@@ -45,8 +46,239 @@
     return (mine.astype(jnp.float32) + layer_scale.astype(jnp.float32) * merged).astype(jnp.bfloat16)
 
 
+LINKS = 4
+
+
+def fused(patches, rows, gain, w_hbm, ow_hbm, scale, pos, out,
+          own, mine, feats, w, ow, w_tail, qkv, att, ret, tmp,
+          load, send, recv):
+    n, per, wide = own.shape
+    cols = patches.shape[1]
+    full = cols // 128 * 128
+    rest = cols - full
+    quarters = feats.shape[0]
+    depth = w.shape[0]
+    heads = w.shape[1] // (3 * HD)
+    hw = heads * HD
+
+    s = lax.axis_index("dp")
+    t = lax.axis_index("tensor")
+    z, core = lax.div(s, 2), lax.rem(s, 2)
+    z_hi, z_lo = lax.div(z, 2), lax.rem(z, 2)
+    y, x = lax.div(t, 2), lax.rem(t, 2)
+    t_x = 2 * y + (1 - x)
+    t_y = 2 * (1 - y) + x
+    t_d = 2 * (1 - y) + (1 - x)
+
+    def chip(j):
+        return 2 * (z_hi if j < 2 else 1 - z_hi) + (z_lo if j % 2 == 0 else 1 - z_lo)
+
+    def peer(k):
+        return 2 * chip(k // 2) + (core if k % 2 == 0 else 1 - core)
+
+    def remote(src, dst, kind, i, o, device):
+        return pltpu.make_async_remote_copy(
+            src_ref=src, dst_ref=dst, send_sem=send.at[kind, i], recv_sem=recv.at[kind, o],
+            device_id=device, device_id_type=MESH)
+
+    barrier = pltpu.get_barrier_semaphore()
+    for k in range(1, n):
+        pl.semaphore_signal(barrier, inc=1, device_id=(peer(k), t), device_id_type=MESH)
+    for other in (t_x, t_y):
+        pl.semaphore_signal(barrier, inc=1, device_id=(s, other), device_id_type=MESH)
+
+    load_w = pltpu.make_async_copy(w_hbm, w, load.at[0])
+    load_ow = pltpu.make_async_copy(ow_hbm, ow, load.at[1])
+    load_w.start()
+    load_ow.start()
+
+    def prepare(d):
+        at = pl.ds(pl.multiple_of(d * per, per), per)
+        idx = lax.rem(rows[pl.ds(d, 1), :], UNIT)
+        hot = lax.broadcasted_iota(jnp.int32, (UNIT, per), 0) == idx
+        hot = jnp.where(hot, 1.0, 0.0).astype(jnp.bfloat16)
+        slot = lax.dot_general(hot, pos[...], (((0,), (0,)), ((), ())), preferred_element_type=jnp.float32)
+        row = (patches[at, :].astype(jnp.float32) + slot).astype(jnp.bfloat16)
+        mine[at, :] = row
+        row = row.astype(jnp.float32)
+        square = jnp.sum(row * row, axis=-1, keepdims=True)
+        scaled = row * gain[...].astype(jnp.float32)
+        tmp[:, full:] = jnp.zeros((per, wide - full), jnp.float32)
+        tmp[:, :cols] = scaled
+        own[d, :, :full] = tmp[:, :full].astype(jnp.bfloat16)
+        first = square.astype(jnp.bfloat16).astype(jnp.float32)
+        second = (square - first).astype(jnp.bfloat16).astype(jnp.float32)
+        third = square - first - second
+        lane = lax.broadcasted_iota(jnp.int32, (per, wide - full), 1)
+        last = jnp.where(lane == rest, first, jnp.where(lane == rest + 1, second, jnp.where(lane == rest + 2, third, tmp[:, full:])))
+        own[d, :, full:] = last.astype(jnp.bfloat16)
+
+    def scatter(buf, src, base, k):
+        d = peer(k)
+        remote(src.at[d], buf.at[t, s], base, d, s, (d, t)).start()
+
+    def direct(buf, base, k):
+        i = peer(k)
+        if k > 0:
+            remote(buf.at[t, i], buf.at[t, i], base, i, i, (s, t)).wait_recv()
+        remote(buf.at[t, i], buf.at[t, i], base + 1, i, i, (s, t_x)).start()
+        remote(buf.at[t, i], buf.at[t, i], base + 2, i, i, (s, t_y)).start()
+
+    def relay(buf, base, k):
+        i = peer(k)
+        remote(buf.at[t, i], buf.at[t_x, i], base + 1, i, i, (s, t_x)).wait_recv()
+        remote(buf.at[t, i], buf.at[t_y, i], base + 2, i, i, (s, t_y)).wait_recv()
+        if k % 2 == 0:
+            remote(buf.at[t_x, i], buf.at[t_x, i], base + 3, i, i, (s, t_y)).start()
+        else:
+            remote(buf.at[t_y, i], buf.at[t_y, i], base + 3, i, i, (s, t_x)).start()
+
+    def settle(buf, base, k):
+        i = peer(k)
+        remote(buf.at[t_d, i], buf.at[t_d, i], base + 3, i, i, (s, t_x)).wait_recv()
+
+    def project(j):
+        settle(feats, 0, 2 * j)
+        settle(feats, 0, 2 * j + 1)
+        zj = chip(j)
+        two = pl.ds(2 * zj, 2)
+        at = pl.ds(pl.multiple_of(zj * 2 * per, 2 * per), 2 * per)
+        lane = lax.broadcasted_iota(jnp.int32, (2 * per, 128), 1)
+        tail = jnp.zeros((2 * per, 128), jnp.float32)
+        square = jnp.zeros((2 * per, 128), jnp.float32)
+        for q in range(quarters):
+            last = feats[q, two, :, full:].reshape(2 * per, 128).astype(jnp.float32)
+            square += jnp.where((lane >= rest) & (lane < rest + 3), last, 0.0)
+            moved = last if q == 0 else pltpu.roll(last, rest * q, 1)
+            tail = jnp.where((lane >= rest * q) & (lane < rest * (q + 1)), moved, tail)
+        tail = tail.astype(jnp.bfloat16)
+        norm = lax.rsqrt(jnp.sum(square, axis=-1, keepdims=True) * (1.0 / depth) + EPS)
+
+        def head(h, carry):
+            span = pl.ds(pl.multiple_of(h * 3 * HD, 128), 3 * HD)
+            acc = jnp.dot(tail, w_tail[:, span], preferred_element_type=jnp.float32)
+            for q in range(quarters):
+                part = feats[q, two, :, :full].reshape(2 * per, full)
+                acc += jnp.dot(part, w[q * cols:q * cols + full, span], preferred_element_type=jnp.float32)
+            qkv[at, span] = (acc * norm).astype(jnp.bfloat16)
+            return carry
+
+        lax.fori_loop(0, heads, head, 0)
+
+    def attend(j):
+        zj = chip(j)
+        at = pl.ds(pl.multiple_of(zj * 2 * per, 2 * per), 2 * per)
+
+        def head(h, carry):
+            q = qkv[at, pl.ds(pl.multiple_of(h * 3 * HD, 128), HD)]
+            k = qkv[:, pl.ds(pl.multiple_of(h * 3 * HD + HD, 128), HD)]
+            v = qkv[:, pl.ds(pl.multiple_of(h * 3 * HD + 2 * HD, 128), HD)]
+            score = lax.dot_general(q, k, (((1,), (1,)), ((), ())), preferred_element_type=jnp.float32)
+            peak = jnp.max(score, axis=-1, keepdims=True)
+            e = jnp.exp2((score - peak) * (HD ** (-0.5) * 1.4426950408889634))
+            total = jnp.sum(e, axis=-1, keepdims=True)
+            o = jnp.dot(e.astype(jnp.bfloat16), v, preferred_element_type=jnp.float32) / total
+            att[pl.ds(2 * zj, 2), :, pl.ds(pl.multiple_of(h * HD, 128), HD)] = o.astype(jnp.bfloat16).reshape(2, per, HD)
+            return carry
+
+        lax.fori_loop(0, heads, head, 0)
+
+    def finish(j):
+        settle(ret, LINKS, 2 * j)
+        settle(ret, LINKS, 2 * j + 1)
+        zj = chip(j)
+        at = pl.ds(pl.multiple_of(zj * 2 * per, 2 * per), 2 * per)
+        acc = jnp.zeros((2 * per, cols), jnp.float32)
+        for q in range(quarters):
+            part = ret[q, pl.ds(2 * zj, 2)].reshape(2 * per, hw)
+            acc += jnp.dot(part, ow[q * hw:(q + 1) * hw, :], preferred_element_type=jnp.float32)
+        out[at, :] = (mine[at, :].astype(jnp.float32) + scale[...].astype(jnp.float32) * acc).astype(jnp.bfloat16)
+
+    prepare(s)
+    feats[t, s] = own[s]
+    pl.semaphore_wait(barrier, n + 1)
+    direct(feats, 0, 0)
+    for k in range(1, n):
+        prepare(peer(k))
+        scatter(feats, own, 0, k)
+    load_w.wait()
+    for q in range(quarters):
+        w_tail[q * rest:(q + 1) * rest, :] = w[q * cols + full:(q + 1) * cols, :]
+    for k in range(1, n):
+        direct(feats, 0, k)
+        relay(feats, 0, k - 1)
+        if k >= 3 and k % 2 == 1:
+            project((k - 3) // 2)
+    relay(feats, 0, n - 1)
+    project(n // 2 - 1)
+
+    pairs = n // 2
+    load_ow.wait()
+    for j in range(pairs + 2):
+        if j < pairs:
+            attend(j)
+            for k in (2 * j, 2 * j + 1):
+                if k == 0:
+                    ret[t, s] = att[s]
+                    direct(ret, LINKS, 0)
+                else:
+                    scatter(ret, att, LINKS, k)
+        if 1 <= j <= pairs:
+            for k in (2 * j - 2, 2 * j - 1):
+                if k > 0:
+                    direct(ret, LINKS, k)
+            for k in (2 * j - 2, 2 * j - 1):
+                relay(ret, LINKS, k)
+        if j >= 2:
+            finish(j - 2)
+
+    for k in range(n):
+        i = peer(k)
+        for base, buf, src in ((0, feats, own), (LINKS, ret, att)):
+            for kind in range(LINKS):
+                if kind > 0 or k > 0:
+                    whole = src.at[i] if kind == 0 else buf.at[t, i]
+                    remote(whole, whole, base + kind, i, i, (s, t_x)).wait_send()
+
+
+def one_kernel(patches, encoder_row, norm_gain, joint_weight, out_weight, layer_scale, pos_embed):
+    n, quarters = lax.axis_size("dp"), lax.axis_size("tensor")
+    rows, cols = patches.shape
+    per = rows // n
+    wide = -(-cols // 128) * 128
+    hw = out_weight.shape[0] // quarters
+    vmem = pl.BlockSpec(memory_space=pltpu.VMEM)
+    hbm = pl.BlockSpec(memory_space=pl.ANY)
+    bf16 = jnp.bfloat16
+    return pl.pallas_call(
+        fused,
+        out_shape=jax.ShapeDtypeStruct((rows, cols), bf16),
+        in_specs=[vmem, vmem, vmem, hbm, hbm, vmem, vmem],
+        out_specs=vmem,
+        scratch_shapes=[
+            pltpu.VMEM((n, per, wide), bf16),
+            pltpu.VMEM((rows, cols), bf16),
+            pltpu.VMEM((quarters, n, per, wide), bf16),
+            pltpu.VMEM(joint_weight.shape, bf16),
+            pltpu.VMEM(out_weight.shape, bf16),
+            pltpu.VMEM((128, joint_weight.shape[1]), bf16),
+            pltpu.VMEM((rows, joint_weight.shape[1]), bf16),
+            pltpu.VMEM((n, per, hw), bf16),
+            pltpu.VMEM((quarters, n, per, hw), bf16),
+            pltpu.VMEM((per, wide), jnp.float32),
+            pltpu.SemaphoreType.DMA((2,)),
+            pltpu.SemaphoreType.DMA((2 * LINKS, n)),
+            pltpu.SemaphoreType.DMA((2 * LINKS, n)),
+        ],
+        compiler_params=pltpu.CompilerParams(
+            collective_id=0, has_side_effects=True, vmem_limit_bytes=60 * 1024 * 1024),
+    )(patches, encoder_row.reshape(n, per), norm_gain.reshape(1, cols), joint_weight, out_weight,
+      layer_scale.reshape(1, cols), pos_embed)
+
+
 def solution(mesh):
-    body = plain
+    fits = dict(mesh.shape) == dict(dp=8, tensor=4)
+    body = one_kernel if fits else plain
     placed = (
         P("dp", "tensor"),
         P("dp"),

time: 304 us -> 148 us (0.49)
  Pallas kernels: 0 us -> 129 us
  waiting for transfers between devices: 110 us -> 0 us
  blocking collectives: 86.6 us -> 0 us
  matrix products: 46.4 us -> 0 us
  other arithmetic: 19.3 us -> 0 us
  between operations: 14.1 us -> 0.01 us
  local copies, waits for them, and re-layouts: 26.3 us -> 17.9 us
    pallas_call x0 -> x1, Pallas kernels: none -> 129 us  [one_kernel(): pl.pallas_call(fused, out_shape=jax.ShapeDtypeStruct((rows, cols), bf16),...]
    all_gather x2 -> x0, waiting for transfers between devices: 110 us -> none  [the longest x1 59.7 us: plain(): lax.all_gather(tile_rows, 'tensor', axis=1, tiled=True).astype(jnp.float32)]
    all_to_all x2 -> x0, blocking collectives: 76.5 us -> none  [swap(): return lax.all_to_all(x, 'dp', split_axis=0, concat_axis=0, tiled=True)]
    dot_general x4 -> x0, matrix products: 46.4 us -> none  [the longest x1 14.8 us: plain(): proj = jnp.dot(scaled, joint_weight, preferred_element_type=jnp.float32)]
    sub x1 -> x0, other arithmetic: 12.6 us -> none  [plain(): e = jnp.exp(scores - jnp.max(scores, axis=-1, keepdims=True))]
    gather x2 -> x0, local copies, waits for them, and re-layouts: 11.2 us -> none  [plain(): pos = pos_embed[encoder_row % UNIT].astype(jnp.float32)]
    unnamed x1 -> x0, blocking collectives: 10.2 us -> none
    unnamed x17 -> x5, local copies, waits for them, and re-layouts: 6.61 us -> 11.6 us
  transfers between devices with their start and end apart: 2 -> 0, of which waited for: 2 -> 0; matrix products, arithmetic and copies ran while one was open for 0% -> 0% of each run, Pallas kernels for 0% -> 0%
where the time goes in v2:
time: 148 us; the launch traced here: 147 us
  Pallas kernels  129 us (87%)
  local copies, waits for them, and re-layouts  17.9 us (12%)
    pallas_call x1, Pallas kernels, one_kernel(): pl.pallas_call(fused, out_shape=jax.ShapeDtypeStruct((rows, cols), bf16),...  129 us
    unnamed x5, local copies, waits for them, and re-layouts  11.6 us
    pallas_call x1, local copies, waits for them, and re-layouts, one_kernel(): pl.pallas_call(fused, out_shape=jax.ShapeDtypeStruct((rows, cols), bf16),...  3.72 us

profile of v2, /device:TPU:0, one launch (start us, length us, event | category | flops | bytes accessed | tf_op | source)
XLA Modules:
  0.0 147.2 jit_solution(1615731493785282545)
XLA Ops:
  0.0 1.3 reshape.10.gain
  1.3 1.3 reshape.11.scale
  2.5 3.7 %copy.8.patches = bf16[1024,800]{1,0:T(8,128)(2,1)} copy(bf16[1024,800]{0,1:T(8,128)(2,1)} %param.7) | data formatting | bytes 3276800 | tf_op args[0]
  6.3 0.0 copy-start
  6.3 3.9 %copy.10.pos = bf16[1024,800]{1,0:T(8,128)(2,1)} copy(bf16[1024,800]{0,1:T(8,128)(2,1)} %param.13) | data formatting | bytes 3276800 | tf_op args[6]
  10.1 0.0 copy-done
  10.1 4.0 %copy.9.ow_hbm = bf16[2048,800]{1,0:T(8,128)(2,1)} copy(bf16[2048,800]{0,1:T(8,128)(2,1)S(1)} %copy-done) | data formatting | bytes 6553600 | tf_op args[4]
  14.2 129.3 %shard_map.73 = bf16[1024,800]{1,0:T(8,128)(2,1)} custom-call(bf16[1024,800]{1,0:T(8,128)(2,1)} %copy.8.patches, s32[8,128]{1,0:T(8,128)} %bitcast.1, bf16[1,800]{1,0:T(2,128)(2,1)} %reshape.10.gain, bf16[3200,1536]{1,0:T(8,128)(2,1)} %w_hbm.1, bf16[2048,800]{1,0:T(8,128)(2,1)} %copy.9.ow_hbm, bf16[1,800]{1,0:T(2,128)(2,1)} %reshape.11.scale, ...), custom_call_target="tpu_custom_call" | custom-call | tf_op jit(solution)/shard_map/pallas_call | solution.py:253
  143.5 3.7 %copy.11 = bf16[1024,800]{0,1:T(8,128)(2,1)} copy(bf16[1024,800]{1,0:T(8,128)(2,1)} %shard_map.73) | data formatting | bytes 3276800 | tf_op jit(solution)/shard_map/pallas_call | solution.py:253
Async XLA Ops:
  6.3 3.9 %copy-start = (bf16[2048,800]{0,1:T(8,128)(2,1)S(1)}, bf16[2048,800]{0,1:T(8,128)(2,1)}, u32[]{:S(2)}) copy-start(bf16[2048,800]{0,1:T(8,128)(2,1)} %param.11) | copy-start | bytes 9830404

commit v3 on v2

--- a/solution.py
+++ b/solution.py
@@ -49,13 +49,16 @@
 LINKS = 4
 
 
-def fused(patches, rows, gain, w_hbm, ow_hbm, scale, pos, out,
-          own, mine, feats, w, ow, w_tail, qkv, att, ret, tmp,
+def fused(patches, rows, sides, w_hbm, ow_hbm, pos, out,
+          own, mine, feats, w, ow, w_tail, qkv, att, ret, gain, scale,
           load, send, recv):
-    n, per, wide = own.shape
-    cols = patches.shape[1]
+    n = own.shape[0]
+    cols = patches.shape[0]
+    per = patches.shape[1] // n
     full = cols // 128 * 128
     rest = cols - full
+    steps = full // 128
+    sums = steps * per + rest
     quarters = feats.shape[0]
     depth = w.shape[0]
     heads = w.shape[1] // (3 * HD)
@@ -92,26 +95,31 @@
     load_w.start()
     load_ow.start()
 
+    for which, wide in enumerate((gain, scale)):
+        pick = lax.broadcasted_iota(jnp.int32, (16, 128), 0) == which
+        pick = jnp.where(pick, 1.0, 0.0).astype(jnp.bfloat16)
+        wide[...] = lax.dot_general(sides[...], pick, (((0,), (0,)), ((), ())), preferred_element_type=jnp.float32)
+
     def prepare(d):
         at = pl.ds(pl.multiple_of(d * per, per), per)
         idx = lax.rem(rows[pl.ds(d, 1), :], UNIT)
         hot = lax.broadcasted_iota(jnp.int32, (UNIT, per), 0) == idx
         hot = jnp.where(hot, 1.0, 0.0).astype(jnp.bfloat16)
-        slot = lax.dot_general(hot, pos[...], (((0,), (0,)), ((), ())), preferred_element_type=jnp.float32)
-        row = (patches[at, :].astype(jnp.float32) + slot).astype(jnp.bfloat16)
-        mine[at, :] = row
+        slot = jnp.dot(pos[...], hot, preferred_element_type=jnp.float32)
+        row = (patches[:, at].astype(jnp.float32) + slot).astype(jnp.bfloat16)
+        mine[:, at] = row
         row = row.astype(jnp.float32)
-        square = jnp.sum(row * row, axis=-1, keepdims=True)
-        scaled = row * gain[...].astype(jnp.float32)
-        tmp[:, full:] = jnp.zeros((per, wide - full), jnp.float32)
-        tmp[:, :cols] = scaled
-        own[d, :, :full] = tmp[:, :full].astype(jnp.bfloat16)
+        square = jnp.sum(row * row, axis=0, keepdims=True)
+        scaled = row * gain[...]
+        for c in range(steps):
+            own[d, c * per:(c + 1) * per, :] = scaled[c * 128:(c + 1) * 128].T.astype(jnp.bfloat16)
+        own[d, steps * per:sums, :] = scaled[full:].astype(jnp.bfloat16)
         first = square.astype(jnp.bfloat16).astype(jnp.float32)
         second = (square - first).astype(jnp.bfloat16).astype(jnp.float32)
         third = square - first - second
-        lane = lax.broadcasted_iota(jnp.int32, (per, wide - full), 1)
-        last = jnp.where(lane == rest, first, jnp.where(lane == rest + 1, second, jnp.where(lane == rest + 2, third, tmp[:, full:])))
-        own[d, :, full:] = last.astype(jnp.bfloat16)
+        at_row = lax.broadcasted_iota(jnp.int32, (16, per), 0)
+        last = jnp.where(at_row == 0, first, jnp.where(at_row == 1, second, jnp.where(at_row == 2, third, 0.0)))
+        own[d, sums:, :] = last.astype(jnp.bfloat16)
 
     def scatter(buf, src, base, k):
         d = peer(k)
@@ -143,22 +151,20 @@
         zj = chip(j)
         two = pl.ds(2 * zj, 2)
         at = pl.ds(pl.multiple_of(zj * 2 * per, 2 * per), 2 * per)
-        lane = lax.broadcasted_iota(jnp.int32, (2 * per, 128), 1)
-        tail = jnp.zeros((2 * per, 128), jnp.float32)
-        square = jnp.zeros((2 * per, 128), jnp.float32)
-        for q in range(quarters):
-            last = feats[q, two, :, full:].reshape(2 * per, 128).astype(jnp.float32)
-            square += jnp.where((lane >= rest) & (lane < rest + 3), last, 0.0)
-            moved = last if q == 0 else pltpu.roll(last, rest * q, 1)
-            tail = jnp.where((lane >= rest * q) & (lane < rest * (q + 1)), moved, tail)
-        tail = tail.astype(jnp.bfloat16)
-        norm = lax.rsqrt(jnp.sum(square, axis=-1, keepdims=True) * (1.0 / depth) + EPS)
+        def sides_of(low, high):
+            return jnp.concatenate(
+                [jnp.concatenate([feats[q, 2 * zj + c, low:high, :] for q in range(quarters)], axis=0) for c in range(2)], axis=1)
+
+        tail = sides_of(steps * per, sums)
+        square = lax.dot_general(sides_of(sums, sums + 16), jnp.ones((16 * quarters, 128), jnp.bfloat16),
+                                 (((0,), (0,)), ((), ())), preferred_element_type=jnp.float32)
+        norm = lax.rsqrt(square[:, :1] * (1.0 / depth) + EPS)
 
         def head(h, carry):
             span = pl.ds(pl.multiple_of(h * 3 * HD, 128), 3 * HD)
-            acc = jnp.dot(tail, w_tail[:, span], preferred_element_type=jnp.float32)
+            acc = lax.dot_general(tail, w_tail[:, span], (((0,), (0,)), ((), ())), preferred_element_type=jnp.float32)
             for q in range(quarters):
-                part = feats[q, two, :, :full].reshape(2 * per, full)
+                part = jnp.concatenate([feats[q, two, c * per:(c + 1) * per, :].reshape(2 * per, 128) for c in range(steps)], axis=1)
                 acc += jnp.dot(part, w[q * cols:q * cols + full, span], preferred_element_type=jnp.float32)
             qkv[at, span] = (acc * norm).astype(jnp.bfloat16)
             return carry
@@ -188,11 +194,12 @@
         settle(ret, LINKS, 2 * j + 1)
         zj = chip(j)
         at = pl.ds(pl.multiple_of(zj * 2 * per, 2 * per), 2 * per)
-        acc = jnp.zeros((2 * per, cols), jnp.float32)
+        acc = jnp.zeros((cols, 2 * per), jnp.float32)
         for q in range(quarters):
             part = ret[q, pl.ds(2 * zj, 2)].reshape(2 * per, hw)
-            acc += jnp.dot(part, ow[q * hw:(q + 1) * hw, :], preferred_element_type=jnp.float32)
-        out[at, :] = (mine[at, :].astype(jnp.float32) + scale[...].astype(jnp.float32) * acc).astype(jnp.bfloat16)
+            acc += lax.dot_general(ow[:, q * hw:(q + 1) * hw], part, (((1,), (1,)), ((), ())), preferred_element_type=jnp.float32)
+        level = jnp.concatenate([scale[...], scale[...]], axis=1)
+        out[:, at] = (mine[:, at].astype(jnp.float32) + level * acc).astype(jnp.bfloat16)
 
     prepare(s)
     feats[t, s] = own[s]
@@ -245,35 +252,37 @@
     n, quarters = lax.axis_size("dp"), lax.axis_size("tensor")
     rows, cols = patches.shape
     per = rows // n
-    wide = -(-cols // 128) * 128
+    packed = cols // 128 * per + cols % 128 + 16
     hw = out_weight.shape[0] // quarters
     vmem = pl.BlockSpec(memory_space=pltpu.VMEM)
     hbm = pl.BlockSpec(memory_space=pl.ANY)
     bf16 = jnp.bfloat16
-    return pl.pallas_call(
+    sides = jnp.pad(jnp.stack([norm_gain, layer_scale]), ((0, 14), (0, 0)))
+    result = pl.pallas_call(
         fused,
-        out_shape=jax.ShapeDtypeStruct((rows, cols), bf16),
-        in_specs=[vmem, vmem, vmem, hbm, hbm, vmem, vmem],
+        out_shape=jax.ShapeDtypeStruct((cols, rows), bf16),
+        in_specs=[vmem, vmem, vmem, hbm, hbm, vmem],
         out_specs=vmem,
         scratch_shapes=[
-            pltpu.VMEM((n, per, wide), bf16),
-            pltpu.VMEM((rows, cols), bf16),
-            pltpu.VMEM((quarters, n, per, wide), bf16),
+            pltpu.VMEM((n, packed, 128), bf16),
+            pltpu.VMEM((cols, rows), bf16),
+            pltpu.VMEM((quarters, n, packed, 128), bf16),
             pltpu.VMEM(joint_weight.shape, bf16),
-            pltpu.VMEM(out_weight.shape, bf16),
+            pltpu.VMEM((cols, quarters * hw), bf16),
             pltpu.VMEM((128, joint_weight.shape[1]), bf16),
             pltpu.VMEM((rows, joint_weight.shape[1]), bf16),
             pltpu.VMEM((n, per, hw), bf16),
             pltpu.VMEM((quarters, n, per, hw), bf16),
-            pltpu.VMEM((per, wide), jnp.float32),
+            pltpu.VMEM((cols, 128), jnp.float32),
+            pltpu.VMEM((cols, 128), jnp.float32),
             pltpu.SemaphoreType.DMA((2,)),
             pltpu.SemaphoreType.DMA((2 * LINKS, n)),
             pltpu.SemaphoreType.DMA((2 * LINKS, n)),
         ],
         compiler_params=pltpu.CompilerParams(
             collective_id=0, has_side_effects=True, vmem_limit_bytes=60 * 1024 * 1024),
-    )(patches, encoder_row.reshape(n, per), norm_gain.reshape(1, cols), joint_weight, out_weight,
-      layer_scale.reshape(1, cols), pos_embed)
+    )(patches.T, encoder_row.reshape(n, per), sides, joint_weight, out_weight.T, pos_embed.T)
+    return result.T
 
 
 def solution(mesh):

time: 148 us -> 130 us (0.88)
  local copies, waits for them, and re-layouts: 17.9 us -> 4.09 us
  Pallas kernels: 129 us -> 125 us
    unnamed x5 -> x1, local copies, waits for them, and re-layouts: 11.6 us -> 2.72 us
    pallas_call x1, Pallas kernels: 129 us -> 125 us  [one_kernel(): pl.pallas_call(fused, out_shape=jax.ShapeDtypeStruct((cols, rows), bf16),...]
    pallas_call x1 -> x0, local copies, waits for them, and re-layouts: 3.72 us -> none  [one_kernel(): pl.pallas_call(fused, out_shape=jax.ShapeDtypeStruct((rows, cols), bf16),...]
    reshape x2 -> x0, local copies, waits for them, and re-layouts: 2.53 us -> none  [the longest x1 1.27 us: one_kernel(): layer_scale.reshape(1, cols)]
where the time goes in v3:
time: 130 us
  Pallas kernels  125 us (96%)
  local copies, waits for them, and re-layouts  4.09 us (3%)
    pallas_call x1, Pallas kernels, one_kernel(): pl.pallas_call(fused, out_shape=jax.ShapeDtypeStruct((cols, rows), bf16),...  125 us
    unnamed x1, local copies, waits for them, and re-layouts  2.72 us

profile of v3, /device:TPU:0, one launch (start us, length us, event | category | flops | bytes accessed | tf_op | source)
XLA Modules:
  0.0 130.1 jit_solution(13810536183898335086)
XLA Ops:
  0.0 0.7 stack.9
  0.7 0.7 stack.10
  1.4 0.6 fusion.2.sides
  2.0 125.4 %shard_map.73 = bf16[800,1024]{1,0:T(8,128)(2,1)} custom-call(bf16[800,1024]{1,0:T(8,128)(2,1)} %bitcast.7, s32[8,128]{1,0:T(8,128)} %bitcast.9, bf16[16,800]{1,0:T(8,128)(2,1)} %fusion.2.sides, bf16[3200,1536]{1,0:T(8,128)(2,1)} %w_hbm.1, bf16[800,2048]{1,0:T(8,128)(2,1)} %bitcast.6, bf16[800,1024]{1,0:T(8,128)(2,1)} %bitcast.8), custom_call_target="tpu_custom_call" | custom-call | tf_op jit(solution)/shard_map/pallas_call | solution.py:261
  127.4 2.7 %copy.9 = bf16[1024,800]{0,1:T(8,128)(2,1)} copy(bf16[1024,800]{0,1:T(8,128)(2,1)} %bitcast.5) | data formatting | bytes 3276800

commit v4 on v3

--- a/solution.py
+++ b/solution.py
@@ -230,9 +230,11 @@
                     direct(ret, LINKS, 0)
                 else:
                     scatter(ret, att, LINKS, k)
+            if j == 0:
+                direct(ret, LINKS, 1)
         if 1 <= j <= pairs:
             for k in (2 * j - 2, 2 * j - 1):
-                if k > 0:
+                if k > 1:
                     direct(ret, LINKS, k)
             for k in (2 * j - 2, 2 * j - 1):
                 relay(ret, LINKS, k)

time: 130 us -> 130 us (level)
  no operation moved by 1% of the time
where the time goes in v4:
time: 130 us
  Pallas kernels  126 us (97%)
  local copies, waits for them, and re-layouts  4.09 us (3%)
    pallas_call x1, Pallas kernels, one_kernel(): pl.pallas_call(fused, out_shape=jax.ShapeDtypeStruct((cols, rows), bf16),...  126 us
    unnamed x1, local copies, waits for them, and re-layouts  2.72 us

profile of v4, /device:TPU:0, one launch (start us, length us, event | category | flops | bytes accessed | tf_op | source)
XLA Modules:
  0.0 130.2 jit_solution(12886471296917460860)
XLA Ops:
  0.0 0.7 stack.9
  0.7 0.7 stack.10
  1.4 0.6 fusion.2.sides
  2.0 125.5 %shard_map.73 = bf16[800,1024]{1,0:T(8,128)(2,1)} custom-call(bf16[800,1024]{1,0:T(8,128)(2,1)} %bitcast.7, s32[8,128]{1,0:T(8,128)} %bitcast.9, bf16[16,800]{1,0:T(8,128)(2,1)} %fusion.2.sides, bf16[3200,1536]{1,0:T(8,128)(2,1)} %w_hbm.1, bf16[800,2048]{1,0:T(8,128)(2,1)} %bitcast.6, bf16[800,1024]{1,0:T(8,128)(2,1)} %bitcast.8), custom_call_target="tpu_custom_call" | custom-call | tf_op jit(solution)/shard_map/pallas_call | solution.py:263
  127.5 2.7 %copy.9 = bf16[1024,800]{0,1:T(8,128)(2,1)} copy(bf16[1024,800]{0,1:T(8,128)(2,1)} %bitcast.5) | data formatting | bytes 3276800
